TPU v7x, 32 devices: a whole 2x2x4 slice. The times are simulated.
32 devices in a mesh: sta: 16 (over z, y, x), stk: 2 (over core).
Axes of the slice: x: 2, y: 2, z: 4, core: 2. Of those that a mesh axis runs over, the one named last changes fastest.
Arguments:
- spectra: float32 [2, 64, 2, 2048], P('stk', 'sta')
- partner_masks: int32 [4], replicated, may hold values from 1 to 15, as said below
Outputs:
- correlations: float32 [256, 4, 2400], P(('sta', 'stk'))
Inputs may be any that keep to these rules, and one draw needn't show every extreme that they name: `partner_masks`: each round's block pairing is b with b XOR mask; every bit below log2 of the number of station blocks is set in some round's mask.
All inputs are finite; a program needn't handle non-finite values.
Results may differ from a plain program's by a relative error of at most 0.0037.
Values may be sent and summed in bfloat16 or wider, within the bound.
A program may use at most 64 MiB of HBM per device.

v0:
```python
import functools
import math

import jax
import jax.numpy as jnp
import ml_dtypes
import numpy as np
from jax import lax
from jax.experimental import pallas as pl
from jax.experimental.pallas import tpu as pltpu
from jax.sharding import PartitionSpec as P

NFFT = 8192
MAXLAG = 1200
LANES = 128
FINE = NFFT // LANES
GROUPS = -(-2 * MAXLAG // LANES)
GROUP_ROWS = -(-GROUPS // 8) * 8
MESH = pl.DeviceIdType.MESH
VMEM = pl.BlockSpec(memory_space=pltpu.VMEM)


def routes(count):
    plan = [(high, 0, high) for high in range(4, count, 4)]
    plan += [(low, 0, low) for low in (1, 2, 3)]
    plan += [(high | low, high, low) for high in range(8, count, 4) for low in (1, 2, 3)]
    plan += [(4 | low, low, 4) for low in (1, 2, 3)]
    return plan


def gather_kernel(
    n_sta, n_stk, x_ref, mask_ref, first_ref, twist_ref, last_ref,
    own_ref, far_ref, first_out, twist_out, last_out,
    x_here, masks, first_here, last_here, stage, slots, load_sem,
    send_sem, recv_sem, own_send, own_recv, far_send, far_recv,
):
    sta = lax.axis_index("sta")
    stk = lax.axis_index("stk")
    plan = routes(n_sta)
    hops = sorted({hop for _, _, hop in plan})
    sources = (x_ref, mask_ref, first_ref, twist_ref, last_ref)
    targets = (x_here, masks, first_here, twist_out, last_here)
    loads = [
        pltpu.make_async_copy(source, target, load_sem.at[index])
        for index, (source, target) in enumerate(zip(sources, targets))
    ]
    for load in loads:
        load.start()
    barrier = pltpu.get_barrier_semaphore()
    for hop in hops:
        pl.semaphore_signal(
            barrier, inc=1, device_id=(jnp.bitwise_xor(sta, hop), stk), device_id_type=MESH
        )
    for other in range(1, n_stk):
        pl.semaphore_signal(
            barrier, inc=1, device_id=(sta, jnp.bitwise_xor(stk, other)), device_id_type=MESH
        )

    loads[0].wait()
    _, stations, _, bins = x_here.shape
    rows = bins // LANES
    for s in range(stations):
        for a in range(rows):
            stage[s, :, a, :] = x_here[0, s, :, a * LANES : (a + 1) * LANES]
    for s in range(stations):
        re = stage[s, 0]
        im = stage[s, 1]
        power = re * re + im * im
        level = jnp.sum(power, keepdims=True) * (1.0 / bins)
        denom = jnp.sqrt(power + 0.05 * (level + 1e-06))
        slots[0, s, 0] = (re / denom).astype(jnp.bfloat16)
        slots[0, s, 1] = (im / denom).astype(jnp.bfloat16)

    pl.semaphore_wait(barrier, len(hops) + n_stk - 1)

    def link(d, parent, hop):
        return pltpu.make_async_remote_copy(
            src_ref=slots.at[parent],
            dst_ref=slots.at[d],
            send_sem=send_sem.at[d],
            recv_sem=recv_sem.at[d],
            device_id=(jnp.bitwise_xor(sta, hop), stk),
            device_id_type=MESH,
        )

    copies = {d: link(d, parent, hop) for d, parent, hop in plan}
    children = {}
    for d, parent, _ in plan:
        children.setdefault(parent, []).append(d)
    for d in children[0]:
        copies[d].start()

    own_ref[stk] = slots[0]
    own_copies = []
    for other in range(1, n_stk):
        peer = (sta, jnp.bitwise_xor(stk, other))
        copy = pltpu.make_async_remote_copy(
            src_ref=slots.at[0],
            dst_ref=own_ref.at[stk],
            send_sem=own_send.at[other],
            recv_sem=own_recv.at[other],
            device_id=peer,
            device_id_type=MESH,
        )
        copy.start()
        own_copies.append(copy)

    for load in loads[1:]:
        load.wait()
    first_out[...] = first_here[...].astype(jnp.bfloat16)
    last_out[...] = last_here[...].astype(jnp.bfloat16)

    for d, _, _ in plan:
        copies[d].wait_recv()
        for child in children.get(d, []):
            copies[child].start()

    far_copies = []
    for r in range(far_ref.shape[1]):
        far_ref[stk, r] = slots[masks[r]]
    for other in range(1, n_stk):
        copy = pltpu.make_async_remote_copy(
            src_ref=far_ref.at[stk],
            dst_ref=far_ref.at[stk],
            send_sem=far_send.at[other],
            recv_sem=far_recv.at[other],
            device_id=(sta, jnp.bitwise_xor(stk, other)),
            device_id_type=MESH,
        )
        copy.start()
        far_copies.append(copy)
    for d, _, _ in plan:
        copies[d].wait_send()
    for copy in own_copies + far_copies:
        copy.wait()


def split(value):
    high = value.astype(jnp.bfloat16)
    low = (value - high.astype(jnp.float32)).astype(jnp.bfloat16)
    return high, low


def transform_kernel(
    n_stk, own_ref, far_ref, first_ref, twist_ref, last_ref, out_ref, joined, turned, lagged
):
    stk = lax.axis_index("stk")
    pairs, rounds, lags = out_ref.shape
    stations = far_ref.shape[2]
    grid = far_ref.shape[4:]
    rows = grid[0]
    bin_index = LANES * lax.broadcasted_iota(jnp.int32, grid, 0) + lax.broadcasted_iota(
        jnp.int32, grid, 1
    )
    weight = jnp.where(bin_index == 0, 0.5, 1.0).astype(jnp.float32)
    lane = lax.broadcasted_iota(jnp.int32, (GROUP_ROWS, LANES), 1)
    for p in range(pairs):
        pair = stk * pairs + p
        i = pair // stations
        j = lax.rem(pair, stations)
        own = [
            [own_ref[w, i, c].astype(jnp.float32) * weight for c in range(2)]
            for w in range(n_stk)
        ]
        for r in range(rounds):
            re = im = None
            for w in range(n_stk):
                ar, ai = own[w]
                br = far_ref[w, r, j, 0].astype(jnp.float32)
                bi = far_ref[w, r, j, 1].astype(jnp.float32)
                re_w = ar * br + ai * bi
                im_w = ai * br - ar * bi
                re = re_w if re is None else re + re_w
                im = im_w if im is None else im + im_w
            re_high, re_low = split(re)
            im_high, im_low = split(im)
            parts = (re_high, im_high, re_low, im_low, re_high, im_high)
            for index, part in enumerate(parts):
                joined[
                    p, index * rows : (index + 1) * rows, r * LANES : (r + 1) * LANES
                ] = part
    for p in range(pairs):
        inner = jnp.dot(first_ref[...], joined[p], preferred_element_type=jnp.float32)
        for r in range(rounds):
            in_re = inner[:FINE, r * LANES : (r + 1) * LANES]
            in_im = inner[FINE:, r * LANES : (r + 1) * LANES]
            here = slice(r * FINE, (r + 1) * FINE)
            for c, value in enumerate(
                (
                    in_re * twist_ref[0] - in_im * twist_ref[1],
                    in_re * twist_ref[1] + in_im * twist_ref[0],
                )
            ):
                high, low = split(value)
                turned[0, p, here, c * LANES : (c + 1) * LANES] = high
                turned[1, p, here, c * LANES : (c + 1) * LANES] = low
    contract = (((1,), (1,)), ((), ()))
    for p in range(pairs):
        both = lax.dot_general(
            last_ref[...], turned[0, p], contract, preferred_element_type=jnp.float32
        )
        rest = lax.dot_general(
            last_ref[: 2 * GROUP_ROWS], turned[1, p], contract,
            preferred_element_type=jnp.float32,
        )
        series = both[: 2 * GROUP_ROWS] + both[2 * GROUP_ROWS :] + rest
        for half in range(rounds // 2):
            even = series[:GROUP_ROWS, half * LANES : (half + 1) * LANES]
            odd = series[GROUP_ROWS:, half * LANES : (half + 1) * LANES]
            base = (p * rounds + 2 * half) * GROUP_ROWS
            lagged[base : base + GROUP_ROWS] = jnp.where(lane < FINE, even, pltpu.roll(odd, FINE, 1))
            lagged[base + GROUP_ROWS : base + 2 * GROUP_ROWS] = jnp.where(
                lane < FINE, pltpu.roll(even, FINE, 1), odd
            )
    for p in range(pairs):
        for g in range(GROUPS):
            span = min(LANES, lags - g * LANES)
            values = lagged[pl.ds(p * rounds * GROUP_ROWS + g, rounds, stride=GROUP_ROWS), :]
            out_ref[p, :, g * LANES : g * LANES + span] = values[:, :span]


def turn(product):
    return np.remainder(product, NFFT) * (2.0 * math.pi / NFFT)


def tables(bins, windows):
    a = np.arange(bins // LANES)
    f = np.arange(FINE)
    c = np.arange(LANES)
    scale = 2.0 / math.sqrt(windows * bins)
    angle = turn(LANES * a[None, :] * (f[:, None] - MAXLAG))
    cos, sin = np.cos(angle), np.sin(angle)
    first = np.block([[cos, -sin], [sin, cos]]).astype(np.float32)
    angle = turn(c[None, :] * (f[:, None] - MAXLAG))
    twist = (np.stack([np.cos(angle), np.sin(angle)]) * scale).astype(np.float32)
    group = np.zeros((2, GROUP_ROWS), np.int64)
    group[0, :GROUPS] = 2 * np.arange(GROUPS)
    group[1, :GROUPS] = 2 * np.arange(GROUPS) + 1
    angle = turn(FINE * group.reshape(-1)[:, None] * c[None, :])
    last = np.concatenate([np.cos(angle), -np.sin(angle)], axis=1).astype(np.float32)

    def halves(table):
        high = table.astype(ml_dtypes.bfloat16).astype(np.float32)
        return high, (table - high).astype(ml_dtypes.bfloat16).astype(np.float32)

    first_high, first_low = halves(first)
    last_high, last_low = halves(last)
    return (
        np.concatenate([first_high, first_high, first_low], axis=1),
        twist,
        np.concatenate([last_high, last_low], axis=0),
    )


def body(n_sta, n_stk, spectra, partner_masks):
    _, stations, parts, bins = spectra.shape
    rounds = partner_masks.shape[0]
    rows = bins // LANES
    block = (stations, parts, rows, LANES)
    fixed = tables(bins, n_stk)
    first_shape, twist_shape, last_shape = [table.shape for table in fixed]
    operands = [
        pltpu.with_memory_space_constraint(jnp.asarray(operand), pltpu.HBM)
        for operand in (spectra, partner_masks, *fixed)
    ]
    own, far, first, twist, last = pl.pallas_call(
        functools.partial(gather_kernel, n_sta, n_stk),
        out_shape=[
            jax.ShapeDtypeStruct((n_stk,) + block, jnp.bfloat16),
            jax.ShapeDtypeStruct((n_stk, rounds) + block, jnp.bfloat16),
            jax.ShapeDtypeStruct(first_shape, jnp.bfloat16),
            jax.ShapeDtypeStruct(twist_shape, jnp.float32),
            jax.ShapeDtypeStruct(last_shape, jnp.bfloat16),
        ],
        in_specs=[pl.BlockSpec(memory_space=pltpu.HBM)] * 5,
        out_specs=[VMEM] * 5,
        scratch_shapes=[
            pltpu.VMEM(spectra.shape, jnp.float32),
            pltpu.SMEM((rounds,), jnp.int32),
            pltpu.VMEM(first_shape, jnp.float32),
            pltpu.VMEM(last_shape, jnp.float32),
            pltpu.VMEM(block, jnp.float32),
            pltpu.VMEM((n_sta,) + block, jnp.bfloat16),
            pltpu.SemaphoreType.DMA((5,)),
            pltpu.SemaphoreType.DMA((n_sta,)),
            pltpu.SemaphoreType.DMA((n_sta,)),
            pltpu.SemaphoreType.DMA((n_stk,)),
            pltpu.SemaphoreType.DMA((n_stk,)),
            pltpu.SemaphoreType.DMA((n_stk,)),
            pltpu.SemaphoreType.DMA((n_stk,)),
        ],
        compiler_params=pltpu.CompilerParams(
            collective_id=0, has_side_effects=True, vmem_limit_bytes=32 * 2**20
        ),
        name="whiten_gather",
    )(*operands)
    pairs = stations * stations // n_stk
    return pl.pallas_call(
        functools.partial(transform_kernel, n_stk),
        out_shape=jax.ShapeDtypeStruct((pairs, rounds, 2 * MAXLAG), jnp.float32),
        in_specs=[VMEM] * 5,
        out_specs=VMEM,
        scratch_shapes=[
            pltpu.VMEM((pairs, 6 * rows, rounds * LANES), jnp.bfloat16),
            pltpu.VMEM((2, pairs, rounds * FINE, 2 * LANES), jnp.bfloat16),
            pltpu.VMEM((pairs * rounds * GROUP_ROWS, LANES), jnp.float32),
        ],
        compiler_params=pltpu.CompilerParams(vmem_limit_bytes=32 * 2**20),
        name="cross_transform",
    )(own, far, first, twist, last)


def solution(mesh):
    return jax.shard_map(
        functools.partial(body, mesh.shape["sta"], mesh.shape["stk"]),
        mesh=mesh,
        in_specs=(P("stk", "sta", None, None), P()),
        out_specs=P(("sta", "stk"), None, None),
        check_vma=False,
    )
```

profile of v0, /device:TPU:0, one launch (start us, length us, event | category | flops | bytes accessed | tf_op | source)
XLA Modules:
  0.0 17.4 jit_solution(5393841352639369401)
XLA Ops:
  0.0 15.1 %whiten_gather.1 = (bf16[2,4,2,16,128]{4,3,2,1,0:T(8,128)(2,1)S(1)}, bf16[2,4,4,2,16,128]{5,4,3,2,1,0:T(8,128)(2,1)S(1)}, bf16[128,96]{1,0:T(8,128)(2,1)S(1)}, f...) custom-call(f32[1,4,2,2048]{3,2,1,0:T(2,128)} %x_ref.1, s32[4]{0:T(128)} %mask_ref.1, f32[128,96]{1,0:T(8,128)} %constant.6.clone.first_ref, ...), custom_call_target="tpu_custom_call" | custom-call | tf_op jit(solution)/shard_map/whiten_gather/pallas_call | solution.py:266
  15.1 2.3 %cross_transform.1 = f32[8,4,2400]{2,1,0:T(4,128)} custom-call(bf16[2,4,2,16,128]{4,3,2,1,0:T(8,128)(2,1)S(1)} %get-tuple-element.10.own_ref, bf16[2,4,4,2,16,128]{5,4,3,2,1,0:T(8,128)(2,1)S(1)} %get-tuple-element.11.far_ref, bf16[128,96]{1,0:T(8,128)(2,1)S(1)} %get-tuple-element.12.first_ref, f32[2,64,128]{2,1,0:T(8,128)S(1)} %get-tuple-element.13.twist_ref, ...), custom_call_target="tpu_custom_call" | custom-call | tf_op jit(solution)/shard_map/cross_transform/pallas_call | solution.py:298
where the time goes:
time: 17.6 us; the launch traced here: 17.4 us
  Pallas kernels  17.4 us (99%)
    pallas_call x1, Pallas kernels, body(): pl.pallas_call(functools.partial(gather_kernel, n_sta, n_stk), out_shape=...  15.1 us
    pallas_call x1, Pallas kernels, body(): pl.pallas_call(functools.partial(transform_kernel, n_stk), out_shape=jax....  2.35 us

commit v1 on v0

--- a/solution.py
+++ b/solution.py
@@ -21,7 +21,7 @@
 
 
 def routes(count):
-    plan = [(high, 0, high) for high in range(4, count, 4)]
+    plan = [(high, 0, high) for high in reversed(range(4, count, 4))]
     plan += [(low, 0, low) for low in (1, 2, 3)]
     plan += [(high | low, high, low) for high in range(8, count, 4) for low in (1, 2, 3)]
     plan += [(4 | low, low, 4) for low in (1, 2, 3)]
@@ -118,17 +118,17 @@
     far_copies = []
     for r in range(far_ref.shape[1]):
         far_ref[stk, r] = slots[masks[r]]
-    for other in range(1, n_stk):
-        copy = pltpu.make_async_remote_copy(
-            src_ref=far_ref.at[stk],
-            dst_ref=far_ref.at[stk],
-            send_sem=far_send.at[other],
-            recv_sem=far_recv.at[other],
-            device_id=(sta, jnp.bitwise_xor(stk, other)),
-            device_id_type=MESH,
-        )
-        copy.start()
-        far_copies.append(copy)
+        for other in range(1, n_stk):
+            copy = pltpu.make_async_remote_copy(
+                src_ref=far_ref.at[stk, r],
+                dst_ref=far_ref.at[stk, r],
+                send_sem=far_send.at[r, other],
+                recv_sem=far_recv.at[r, other],
+                device_id=(sta, jnp.bitwise_xor(stk, other)),
+                device_id_type=MESH,
+            )
+            copy.start()
+            far_copies.append(copy)
     for d, _, _ in plan:
         copies[d].wait_send()
     for copy in own_copies + far_copies:
@@ -191,19 +191,13 @@
                     in_re * twist_ref[1] + in_im * twist_ref[0],
                 )
             ):
-                high, low = split(value)
-                turned[0, p, here, c * LANES : (c + 1) * LANES] = high
-                turned[1, p, here, c * LANES : (c + 1) * LANES] = low
+                turned[p, here, c * LANES : (c + 1) * LANES] = value.astype(jnp.bfloat16)
     contract = (((1,), (1,)), ((), ()))
     for p in range(pairs):
         both = lax.dot_general(
-            last_ref[...], turned[0, p], contract, preferred_element_type=jnp.float32
-        )
-        rest = lax.dot_general(
-            last_ref[: 2 * GROUP_ROWS], turned[1, p], contract,
-            preferred_element_type=jnp.float32,
-        )
-        series = both[: 2 * GROUP_ROWS] + both[2 * GROUP_ROWS :] + rest
+            last_ref[...], turned[p], contract, preferred_element_type=jnp.float32
+        )
+        series = both[: 2 * GROUP_ROWS] + both[2 * GROUP_ROWS :]
         for half in range(rounds // 2):
             even = series[:GROUP_ROWS, half * LANES : (half + 1) * LANES]
             odd = series[GROUP_ROWS:, half * LANES : (half + 1) * LANES]
@@ -286,8 +280,8 @@
             pltpu.SemaphoreType.DMA((n_sta,)),
             pltpu.SemaphoreType.DMA((n_stk,)),
             pltpu.SemaphoreType.DMA((n_stk,)),
-            pltpu.SemaphoreType.DMA((n_stk,)),
-            pltpu.SemaphoreType.DMA((n_stk,)),
+            pltpu.SemaphoreType.DMA((rounds, n_stk)),
+            pltpu.SemaphoreType.DMA((rounds, n_stk)),
         ],
         compiler_params=pltpu.CompilerParams(
             collective_id=0, has_side_effects=True, vmem_limit_bytes=32 * 2**20
@@ -302,7 +296,7 @@
         out_specs=VMEM,
         scratch_shapes=[
             pltpu.VMEM((pairs, 6 * rows, rounds * LANES), jnp.bfloat16),
-            pltpu.VMEM((2, pairs, rounds * FINE, 2 * LANES), jnp.bfloat16),
+            pltpu.VMEM((pairs, rounds * FINE, 2 * LANES), jnp.bfloat16),
             pltpu.VMEM((pairs * rounds * GROUP_ROWS, LANES), jnp.float32),
         ],
         compiler_params=pltpu.CompilerParams(vmem_limit_bytes=32 * 2**20),

time: 17.6 us -> 17.1 us (0.972)
  Pallas kernels: 17.4 us -> 17 us
    pallas_call x1, Pallas kernels: 2.35 us -> 1.88 us  [body(): pl.pallas_call(functools.partial(transform_kernel, n_stk), out_shape=jax....]
where the time goes in v1:
time: 17.1 us; the launch traced here: 17 us
  Pallas kernels  17 us (99%)
    pallas_call x1, Pallas kernels, body(): pl.pallas_call(functools.partial(gather_kernel, n_sta, n_stk), out_shape=...  15.1 us
    pallas_call x1, Pallas kernels, body(): pl.pallas_call(functools.partial(transform_kernel, n_stk), out_shape=jax....  1.88 us

profile of v1, /device:TPU:0, one launch (start us, length us, event | category | flops | bytes accessed | tf_op | source)
XLA Modules:
  0.0 17.0 jit_solution(2779974168651369557)
XLA Ops:
  0.0 15.1 %whiten_gather.1 = (bf16[2,4,2,16,128]{4,3,2,1,0:T(8,128)(2,1)S(1)}, bf16[2,4,4,2,16,128]{5,4,3,2,1,0:T(8,128)(2,1)S(1)}, bf16[128,96]{1,0:T(8,128)(2,1)S(1)}, f...) custom-call(f32[1,4,2,2048]{3,2,1,0:T(2,128)} %x_ref.1, s32[4]{0:T(128)} %mask_ref.1, f32[128,96]{1,0:T(8,128)} %constant.6.clone.first_ref, ...), custom_call_target="tpu_custom_call" | custom-call | tf_op jit(solution)/shard_map/whiten_gather/pallas_call | solution.py:260
  15.1 1.9 %cross_transform.1 = f32[8,4,2400]{2,1,0:T(4,128)} custom-call(bf16[2,4,2,16,128]{4,3,2,1,0:T(8,128)(2,1)S(1)} %get-tuple-element.10.own_ref, bf16[2,4,4,2,16,128]{5,4,3,2,1,0:T(8,128)(2,1)S(1)} %get-tuple-element.11.far_ref, bf16[128,96]{1,0:T(8,128)(2,1)S(1)} %get-tuple-element.12.first_ref, f32[2,64,128]{2,1,0:T(8,128)S(1)} %get-tuple-element.13.twist_ref, ...), custom_call_target="tpu_custom_call" | custom-call | tf_op jit(solution)/shard_map/cross_transform/pallas_call | solution.py:292

commit v2 on v1

--- a/solution.py
+++ b/solution.py
@@ -20,12 +20,10 @@
 VMEM = pl.BlockSpec(memory_space=pltpu.VMEM)
 
 
-def routes(count):
-    plan = [(high, 0, high) for high in reversed(range(4, count, 4))]
-    plan += [(low, 0, low) for low in (1, 2, 3)]
-    plan += [(high | low, high, low) for high in range(8, count, 4) for low in (1, 2, 3)]
-    plan += [(4 | low, low, 4) for low in (1, 2, 3)]
-    return plan
+def zipped(first, second):
+    turns = min(len(first), len(second))
+    mixed = [item for pair in zip(first, second) for item in pair]
+    return mixed + first[turns:] + second[turns:]
 
 
 def gather_kernel(
@@ -36,8 +34,10 @@
 ):
     sta = lax.axis_index("sta")
     stk = lax.axis_index("stk")
-    plan = routes(n_sta)
-    hops = sorted({hop for _, _, hop in plan})
+    core = lax.rem(stk, 2)
+    highs = list(range(8, n_sta, 4)) + [4]
+    lows = [1, 2, 3]
+    hops = highs + lows
     sources = (x_ref, mask_ref, first_ref, twist_ref, last_ref)
     targets = (x_here, masks, first_here, twist_out, last_here)
     loads = [
@@ -73,9 +73,9 @@
 
     pl.semaphore_wait(barrier, len(hops) + n_stk - 1)
 
-    def link(d, parent, hop):
+    def link(d, hop):
         return pltpu.make_async_remote_copy(
-            src_ref=slots.at[parent],
+            src_ref=slots.at[jnp.bitwise_xor(d, hop)],
             dst_ref=slots.at[d],
             send_sem=send_sem.at[d],
             recv_sem=recv_sem.at[d],
@@ -83,12 +83,12 @@
             device_id_type=MESH,
         )
 
-    copies = {d: link(d, parent, hop) for d, parent, hop in plan}
-    children = {}
-    for d, parent, _ in plan:
-        children.setdefault(parent, []).append(d)
-    for d in children[0]:
-        copies[d].start()
+    def start_in_turns(base, even_order, odd_order):
+        for even, odd in zip(even_order, odd_order):
+            hop = even + core * (odd - even)
+            link(base + hop, hop).start()
+
+    start_in_turns(0, zipped(highs, lows), zipped(lows, highs))
 
     own_ref[stk] = slots[0]
     own_copies = []
@@ -110,10 +110,22 @@
     first_out[...] = first_here[...].astype(jnp.bfloat16)
     last_out[...] = last_here[...].astype(jnp.bfloat16)
 
-    for d, _, _ in plan:
-        copies[d].wait_recv()
-        for child in children.get(d, []):
-            copies[child].start()
+    for high in highs[:-1]:
+        link(high, high).wait_recv()
+        start_in_turns(high, [1, 3, 2], [2, 1, 3])
+        if high == 8:
+            link(1, 1).wait_recv()
+            link(5, 4).start()
+    for low in lows:
+        if low > 1:
+            link(low, low).wait_recv()
+            link(4 | low, 4).start()
+    link(4, 4).wait_recv()
+    for low in lows:
+        link(4 | low, 4).wait_recv()
+    for high in highs[:-1]:
+        for low in lows:
+            link(high | low, low).wait_recv()
 
     far_copies = []
     for r in range(far_ref.shape[1]):
@@ -129,8 +141,8 @@
             )
             copy.start()
             far_copies.append(copy)
-    for d, _, _ in plan:
-        copies[d].wait_send()
+    for d in range(1, n_sta):
+        link(d, d).wait_send()
     for copy in own_copies + far_copies:
         copy.wait()
 

time: 17.1 us -> 17 us (level)
  Pallas kernels: 17 us -> 16.8 us
where the time goes in v2:
time: 17 us; the launch traced here: 16.8 us
  Pallas kernels  16.8 us (99%)
    pallas_call x1, Pallas kernels, body(): pl.pallas_call(functools.partial(gather_kernel, n_sta, n_stk), out_shape=...  15 us
    pallas_call x1, Pallas kernels, body(): pl.pallas_call(functools.partial(transform_kernel, n_stk), out_shape=jax....  1.88 us

profile of v2, /device:TPU:0, one launch (start us, length us, event | category | flops | bytes accessed | tf_op | source)
XLA Modules:
  0.0 16.8 jit_solution(6230741908705584858)
XLA Ops:
  0.0 15.0 %whiten_gather.1 = (bf16[2,4,2,16,128]{4,3,2,1,0:T(8,128)(2,1)S(1)}, bf16[2,4,4,2,16,128]{5,4,3,2,1,0:T(8,128)(2,1)S(1)}, bf16[128,96]{1,0:T(8,128)(2,1)S(1)}, f...) custom-call(f32[1,4,2,2048]{3,2,1,0:T(2,128)} %x_ref.1, s32[4]{0:T(128)} %mask_ref.1, f32[128,96]{1,0:T(8,128)} %constant.6.clone.first_ref, ...), custom_call_target="tpu_custom_call" | custom-call | tf_op jit(solution)/shard_map/whiten_gather/pallas_call | solution.py:272
  15.0 1.9 %cross_transform.1 = f32[8,4,2400]{2,1,0:T(4,128)} custom-call(bf16[2,4,2,16,128]{4,3,2,1,0:T(8,128)(2,1)S(1)} %get-tuple-element.10.own_ref, bf16[2,4,4,2,16,128]{5,4,3,2,1,0:T(8,128)(2,1)S(1)} %get-tuple-element.11.far_ref, bf16[128,96]{1,0:T(8,128)(2,1)S(1)} %get-tuple-element.12.first_ref, f32[2,64,128]{2,1,0:T(8,128)S(1)} %get-tuple-element.13.twist_ref, ...), custom_call_target="tpu_custom_call" | custom-call | tf_op jit(solution)/shard_map/cross_transform/pallas_call | solution.py:304

commit v3 on v1

--- a/solution.py
+++ b/solution.py
@@ -22,8 +22,8 @@
 
 def routes(count):
     plan = [(high, 0, high) for high in reversed(range(4, count, 4))]
-    plan += [(low, 0, low) for low in (1, 2, 3)]
-    plan += [(high | low, high, low) for high in range(8, count, 4) for low in (1, 2, 3)]
+    plan += [(low, 0, low) for low in (3, 1, 2)]
+    plan += [(high | low, high, low) for high in range(8, count, 4) for low in (3, 1, 2)]
     plan += [(4 | low, low, 4) for low in (1, 2, 3)]
     return plan
 

time: 17.1 us -> 16.8 us (0.982)
  Pallas kernels: 17 us -> 16.6 us
    pallas_call x1, Pallas kernels: 15.1 us -> 14.7 us  [body(): pl.pallas_call(functools.partial(gather_kernel, n_sta, n_stk), out_shape=...]
where the time goes in v3:
time: 16.8 us; the launch traced here: 16.6 us
  Pallas kernels  16.6 us (99%)
    pallas_call x1, Pallas kernels, body(): pl.pallas_call(functools.partial(gather_kernel, n_sta, n_stk), out_shape=...  14.7 us
    pallas_call x1, Pallas kernels, body(): pl.pallas_call(functools.partial(transform_kernel, n_stk), out_shape=jax....  1.88 us

profile of v3, /device:TPU:0, one launch (start us, length us, event | category | flops | bytes accessed | tf_op | source)
XLA Modules:
  0.0 16.6 jit_solution(5386572226057742174)
XLA Ops:
  0.0 14.7 %whiten_gather.1 = (bf16[2,4,2,16,128]{4,3,2,1,0:T(8,128)(2,1)S(1)}, bf16[2,4,4,2,16,128]{5,4,3,2,1,0:T(8,128)(2,1)S(1)}, bf16[128,96]{1,0:T(8,128)(2,1)S(1)}, f...) custom-call(f32[1,4,2,2048]{3,2,1,0:T(2,128)} %x_ref.1, s32[4]{0:T(128)} %mask_ref.1, f32[128,96]{1,0:T(8,128)} %constant.6.clone.first_ref, ...), custom_call_target="tpu_custom_call" | custom-call | tf_op jit(solution)/shard_map/whiten_gather/pallas_call | solution.py:260
  14.7 1.9 %cross_transform.1 = f32[8,4,2400]{2,1,0:T(4,128)} custom-call(bf16[2,4,2,16,128]{4,3,2,1,0:T(8,128)(2,1)S(1)} %get-tuple-element.10.own_ref, bf16[2,4,4,2,16,128]{5,4,3,2,1,0:T(8,128)(2,1)S(1)} %get-tuple-element.11.far_ref, bf16[128,96]{1,0:T(8,128)(2,1)S(1)} %get-tuple-element.12.first_ref, f32[2,64,128]{2,1,0:T(8,128)S(1)} %get-tuple-element.13.twist_ref, ...), custom_call_target="tpu_custom_call" | custom-call | tf_op jit(solution)/shard_map/cross_transform/pallas_call | solution.py:292
